TPU v7x, 32 devices: a whole 2x2x4 slice. The times are simulated.
32 devices in a mesh: wide: 8 (over z, y), narrow: 4 (over x, core).
Axes of the slice: x: 2, y: 2, z: 4, core: 2. Of those that a mesh axis runs over, the one named last changes fastest.
Arguments:
- hidden: bfloat16 [32768, 768], P(('wide', 'narrow')), may hold values from -6 to 6
- segment: int32 [64, 512], P(('wide', 'narrow')), may hold values from 0 to 3, never falling along the last dimension, each value on 1 to 256 neighbouring positions
- w_qkv: bfloat16 [768, 2304], P('wide', 'narrow'), may hold values from -0.21875 to 0.21875
- w_out: bfloat16 [768, 768], P('wide', 'narrow'), may hold values from -0.875 to 0.875
- w_in: bfloat16 [768, 3072], P('wide', 'narrow'), may hold values from -0.21875 to 0.21875
- w_back: bfloat16 [3072, 768], P('wide', 'narrow'), may hold values from -0.109375 to 0.109375
- vectors: float32 [9216], P(('wide', 'narrow')), may hold values from -0.5 to 1.4, as said below
- cotangent: bfloat16 [32768, 768], P(('wide', 'narrow')), may hold values from -6 to 6
Outputs:
- output: bfloat16 [32768, 768], P(('wide', 'narrow'))
- grad_hidden: float32 [32768, 768], P(('wide', 'narrow'))
- grad_w_qkv: float32 [768, 2304], P('wide', 'narrow')
- grad_w_out: float32 [768, 768], P('wide', 'narrow')
- grad_w_in: float32 [768, 3072], P('wide', 'narrow')
- grad_w_back: float32 [3072, 768], P('wide', 'narrow')
- grad_vectors: float32 [9216], P(('wide', 'narrow'))
Inputs may be any that keep to these rules, and one draw needn't show every extreme that they name: segment numbers never fall along a packed row; each document covers 1 to 256 tokens. `vectors`: the gains lie from 0.6 to 1.4, the biases and shifts from -0.5 to 0.5.
All inputs are finite; a program needn't handle non-finite values.
Results may differ from a plain program's by a relative error of at most 0.015.
Values may be sent and summed in bfloat16 or wider, within the bound.
No kernel may reach another device: no remote copies, remote signals or barrier semaphores. Data moves between devices by JAX's collectives and lax.ppermute only.
A program may use at most 192 MiB of HBM per device.

v0:
```python
import jax
import jax.numpy as jnp
from jax import lax
from jax.sharding import PartitionSpec as P

D = 768
HEADS = 12
FF = 3072


epsilon = 1e-06


def split_vectors(vectors):
    return (
        vectors[0:D],
        vectors[D : 2 * D],
        vectors[2 * D : 3 * D],
        vectors[3 * D : 4 * D],
        vectors[4 * D : 5 * D],
        vectors[5 * D : 5 * D + FF],
        vectors[5 * D + FF : 6 * D + FF],
        vectors[6 * D + FF : 7 * D + FF],
        vectors[7 * D + FF : 8 * D + FF],
    )


def normalize(values):
    center = values - jnp.mean(values, -1, keepdims=True)
    inverse = lax.rsqrt(jnp.mean(center * center, -1, keepdims=True) + epsilon)
    return (center * inverse, inverse)


def normalize_back(grad_norm, normed, inverse):
    return inverse * (
        grad_norm
        - jnp.mean(grad_norm, -1, keepdims=True)
        - normed * jnp.mean(grad_norm * normed, -1, keepdims=True)
    )


def contract_rows(left_side, right_side):
    return lax.dot_general(
        left_side, right_side, (((0,), (0,)), ((), ())), preferred_element_type=jnp.float32
    )


def contract_cols(left_side, right_side):
    return lax.dot_general(
        left_side, right_side, (((1,), (1,)), ((), ())), preferred_element_type=jnp.float32
    )


def smooth(values):
    return jax.nn.gelu(values, approximate=False)


def unpack(packed):
    length = packed.shape[0]
    head_dim = packed.shape[1] // (3 * HEADS)
    shaped = packed.reshape(length, 3, HEADS, head_dim)
    return (shaped[:, 0], shaped[:, 1], shaped[:, 2])


def masked_scores(queries, key_rows, segment_row):
    score_scale = queries.shape[-1] ** (-0.5)
    scores = (
        jnp.einsum("qhd,khd->hqk", queries, key_rows, preferred_element_type=jnp.float32)
        * score_scale
    )
    same_segment = segment_row[:, None] == segment_row[None, :]
    return jnp.where(same_segment[None], scores, -1000000000.0)


def attend(block_item):
    packed, segment_row = block_item
    queries, key_rows, value_rows = unpack(packed)
    scores = masked_scores(queries, key_rows, segment_row)
    largest = jnp.max(scores, -1, keepdims=True)
    weights = jnp.exp(scores - largest)
    totals = jnp.sum(weights, -1, keepdims=True)
    probs_low = (weights / totals).astype(jnp.bfloat16)
    attended = jnp.einsum("hqk,khd->qhd", probs_low, value_rows, preferred_element_type=jnp.float32)
    logsum = (largest + jnp.log(totals))[..., 0]
    return (attended.reshape(packed.shape[0], -1).astype(jnp.bfloat16), logsum)


def attend_back(block_item):
    packed, segment_row, logsum, grad_att = block_item
    queries, key_rows, value_rows = unpack(packed)
    score_scale = queries.shape[-1] ** (-0.5)
    scores = masked_scores(queries, key_rows, segment_row)
    probs = jnp.exp(scores - logsum[..., None])
    grad_heads = grad_att.reshape(queries.shape)
    grad_probs = jnp.einsum(
        "qhd,khd->hqk", grad_heads, value_rows, preferred_element_type=jnp.float32
    )
    inner_sum = jnp.sum(probs * grad_probs, -1, keepdims=True)
    grad_scores = (probs * (grad_probs - inner_sum)).astype(jnp.bfloat16)
    grad_query = (
        jnp.einsum("hqk,khd->qhd", grad_scores, key_rows, preferred_element_type=jnp.float32)
        * score_scale
    )
    grad_key = (
        jnp.einsum("hqk,qhd->khd", grad_scores, queries, preferred_element_type=jnp.float32)
        * score_scale
    )
    grad_value = jnp.einsum(
        "hqk,qhd->khd", probs.astype(jnp.bfloat16), grad_heads, preferred_element_type=jnp.float32
    )
    return jnp.stack([grad_query, grad_key, grad_value], 1).reshape(packed.shape[0], -1)


def per_device(hidden, segment, w_qkv, w_out, w_in, w_back, vectors, cotangent):
    columns = (
        lax.all_gather(w_qkv, "narrow", axis=1, tiled=True),
        lax.all_gather(w_out, "narrow", axis=1, tiled=True),
        lax.all_gather(w_in, "narrow", axis=1, tiled=True),
        lax.all_gather(w_back, "narrow", axis=1, tiled=True),
    )
    weights_full = (
        lax.all_gather(columns[0], "wide", axis=0, tiled=True),
        lax.all_gather(columns[1], "wide", axis=0, tiled=True),
        lax.all_gather(columns[2], "wide", axis=0, tiled=True),
        lax.all_gather(columns[3], "wide", axis=0, tiled=True),
    )
    all_vectors = lax.all_gather(vectors, ("wide", "narrow"), axis=0, tiled=True)
    (
        bias_query,
        bias_value,
        bias_out,
        gain_first,
        shift_first,
        bias_inner,
        bias_back,
        gain_second,
        shift_second,
    ) = split_vectors(all_vectors)
    rows_dev = segment.shape[0]
    length = segment.shape[1]
    projected = jnp.dot(hidden, weights_full[0], preferred_element_type=jnp.float32)
    qkv_bias = jnp.concatenate([bias_query, jnp.zeros((D,), jnp.float32), bias_value])
    packed = (projected + qkv_bias).astype(jnp.bfloat16)
    packed_rows = packed.reshape(rows_dev, length, 3 * D)
    attended, logsum = lax.map(attend, (packed_rows, segment))
    attended = attended.reshape(rows_dev * length, D)
    branch = jnp.dot(attended, weights_full[1], preferred_element_type=jnp.float32) + bias_out
    first_normed, first_inverse = normalize(hidden.astype(jnp.float32) + branch)
    first_out = first_normed * gain_first + shift_first
    first_low = first_out.astype(jnp.bfloat16)
    inner_act = jnp.dot(first_low, weights_full[2], preferred_element_type=jnp.float32) + bias_inner
    activated, gelu_back = jax.vjp(smooth, inner_act)
    activated_low = activated.astype(jnp.bfloat16)
    outward = (
        jnp.dot(activated_low, weights_full[3], preferred_element_type=jnp.float32) + bias_back
    )
    second_normed, second_inverse = normalize(first_out + outward)
    output = (second_normed * gain_second + shift_second).astype(jnp.bfloat16)
    columns_back = (
        lax.all_gather(w_qkv, "narrow", axis=1, tiled=True),
        lax.all_gather(w_out, "narrow", axis=1, tiled=True),
        lax.all_gather(w_in, "narrow", axis=1, tiled=True),
        lax.all_gather(w_back, "narrow", axis=1, tiled=True),
    )
    weights_back = (
        lax.all_gather(columns_back[0], "wide", axis=0, tiled=True),
        lax.all_gather(columns_back[1], "wide", axis=0, tiled=True),
        lax.all_gather(columns_back[2], "wide", axis=0, tiled=True),
        lax.all_gather(columns_back[3], "wide", axis=0, tiled=True),
    )
    grad_output = cotangent.astype(jnp.float32)
    grad_gain_second = jnp.sum(grad_output * second_normed, 0)
    grad_shift_second = jnp.sum(grad_output, 0)
    grad_second = normalize_back(grad_output * gain_second, second_normed, second_inverse)
    grad_bias_back = jnp.sum(grad_second, 0)
    second_low = grad_second.astype(jnp.bfloat16)
    grad_w_back = contract_rows(activated_low, second_low)
    grad_activated = contract_cols(second_low, weights_back[3])
    grad_inner = gelu_back(grad_activated)[0]
    grad_bias_inner = jnp.sum(grad_inner, 0)
    inner_low = grad_inner.astype(jnp.bfloat16)
    grad_w_in = contract_rows(first_low, inner_low)
    grad_first = grad_second + contract_cols(inner_low, weights_back[2])
    grad_gain_first = jnp.sum(grad_first * first_normed, 0)
    grad_shift_first = jnp.sum(grad_first, 0)
    grad_branch = normalize_back(grad_first * gain_first, first_normed, first_inverse)
    grad_bias_out = jnp.sum(grad_branch, 0)
    branch_low = grad_branch.astype(jnp.bfloat16)
    grad_w_out = contract_rows(attended, branch_low)
    grad_att = contract_cols(branch_low, weights_back[1]).astype(jnp.bfloat16)
    grad_packed = lax.map(
        attend_back, (packed_rows, segment, logsum, grad_att.reshape(rows_dev, length, D))
    )
    grad_packed = grad_packed.reshape(rows_dev * length, 3 * D)
    grad_bias_query = jnp.sum(grad_packed[:, :D], 0)
    grad_bias_value = jnp.sum(grad_packed[:, 2 * D :], 0)
    packed_low = grad_packed.astype(jnp.bfloat16)
    grad_w_qkv = contract_rows(hidden, packed_low)
    grad_hidden = grad_branch + contract_cols(packed_low, weights_back[0])
    grad_all_vectors = jnp.concatenate(
        [
            grad_bias_query,
            grad_bias_value,
            grad_bias_out,
            grad_gain_first,
            grad_shift_first,
            grad_bias_inner,
            grad_bias_back,
            grad_gain_second,
            grad_shift_second,
        ]
    )
    own_vectors = lax.psum_scatter(
        grad_all_vectors, ("wide", "narrow"), scatter_dimension=0, tiled=True
    )
    row_sums = (
        lax.psum_scatter(grad_w_qkv, "wide", scatter_dimension=0, tiled=True),
        lax.psum_scatter(grad_w_out, "wide", scatter_dimension=0, tiled=True),
        lax.psum_scatter(grad_w_in, "wide", scatter_dimension=0, tiled=True),
        lax.psum_scatter(grad_w_back, "wide", scatter_dimension=0, tiled=True),
    )
    owned_grads = (
        lax.psum_scatter(
            row_sums[0].astype(jnp.bfloat16), "narrow", scatter_dimension=1, tiled=True
        ).astype(jnp.float32),
        lax.psum_scatter(
            row_sums[1].astype(jnp.bfloat16), "narrow", scatter_dimension=1, tiled=True
        ).astype(jnp.float32),
        lax.psum_scatter(
            row_sums[2].astype(jnp.bfloat16), "narrow", scatter_dimension=1, tiled=True
        ).astype(jnp.float32),
        lax.psum_scatter(
            row_sums[3].astype(jnp.bfloat16), "narrow", scatter_dimension=1, tiled=True
        ).astype(jnp.float32),
    )
    return (
        output,
        grad_hidden,
        owned_grads[0],
        owned_grads[1],
        owned_grads[2],
        owned_grads[3],
        own_vectors,
    )


def solution(mesh):
    return jax.shard_map(
        per_device,
        mesh=mesh,
        in_specs=(
            P(("wide", "narrow"), None),
            P(("wide", "narrow"), None),
            P("wide", "narrow"),
            P("wide", "narrow"),
            P("wide", "narrow"),
            P("wide", "narrow"),
            P(("wide", "narrow")),
            P(("wide", "narrow"), None),
        ),
        out_specs=(
            P(("wide", "narrow"), None),
            P(("wide", "narrow"), None),
            P("wide", "narrow"),
            P("wide", "narrow"),
            P("wide", "narrow"),
            P("wide", "narrow"),
            P(("wide", "narrow")),
        ),
        check_vma=False,
    )
```

profile of v0, /device:TPU:0, one launch (start us, length us, event | category | flops | bytes accessed | tf_op | source)
XLA Modules:
  0.0 1003.7 jit_solution(10007287658321204084)
XLA Ops:
  7.3 8.8 all-gather
  25.0 8.1 all_gather.40
  33.1 8.1 all_gather.42
  41.6 43.0 %all-reduce = f32[9216]{0:T(1024)S(1)} all-reduce(f32[9216]{0:T(1024)S(1)} %dynamic-update-slice), channel_id=1, replica_groups=mesh['wide'=8,'narrow'=4] {'wide','narrow'}, use_global_device_ids=true, to_apply=%add | all-reduce | flops 9216 | bytes 73728
  90.1 8.5 add_convert_fusion
  105.2 23.4 %while.22 = (s32[]{:T(128)}, bf16[2,512,768]{2,1,0:T(8,128)(2,1)}, f32[2,12,512]{2,1,0:T(8,128)S(1)}, bf16[2,512,2304]{1,2,0:T(8,128)(2,1)}, s32[2,512]{1,0:T(2,128)S(1)}, /*index=5*/s32[]{:T(128)}) while((s32[]{:T(128)}, bf16[2,512,768]{2,1,0:T(8,128)(2,1)}, f32[2,12,512]{2,1,0:T(8,128)S(1)}, bf16[2,512,2304]{1,2,0:T(8,128)(2,1)}, ...), condition=%wide.region_3.4_spmd, body=%wide.region_0.3_spmd.sunk | while | flops 843704320 | bytes 50051164 | solution.py:145
  132.9 74.4 %all-gather.10.cloned.1.call-done = bf16[768,3072]{1,0:T(8,128)(2,1)} async-done(((bf16[96,3072]{1,0:T(8,128)(2,1)}), bf16[768,3072]{1,0:T(8,128)(2,1)}) %all-gather.10.cloned.1.call-update) | async-done | bytes 4718608 | tf_op jit(solution)/shard_map/all_gather | solution.py:124
  207.4 37.6 %multiply_convert_fusion.1 = (bf16[1024,3072]{1,0:T(8,128)(2,1)}, f32[1024,3072]{1,0:T(8,128)}, f32[1024,3072]{1,0:T(8,128)}) fusion(f32[3072]{0:T(1024)S(1)} %copy-done.34, bf16[768,3072]{1,0:T(8,128)(2,1)} %all-gather.10.cloned.1.call-done, f32[1024,768]{0,1:T(8,128)S(1)} %get-tuple-element.193, f32[768]{0:T(1024)S(1)} %copy-done.35, ...), kind=kOutput, calls=%fused_computation.44 | convolution fusion | flops 5043388416 | bytes 39348224 | tf_op jit(solution)/shard_map/dot_general | solution.py:151
  245.0 43.5 %all-gather.12.cloned.1.call-done = bf16[3072,768]{0,1:T(8,128)(2,1)} async-done(((bf16[384,768]{0,1:T(8,128)(2,1)}), bf16[3072,768]{0,1:T(8,128)(2,1)}) %all-gather.12.cloned.1.call-update) | async-done | bytes 4718608 | tf_op jit(solution)/shard_map/all_gather | solution.py:125
  288.4 9.2 fusion.61
  301.0 19.3 %fusion.62 = (f32[3072]{0:T(1024)}, bf16[1024,3072]{1,0:T(8,128)(2,1)}) fusion(f32[1024,3072]{1,0:T(8,128)} %get-tuple-element.178, bf16[3072,768]{0,1:T(8,128)(2,1)} %all-gather.12.cloned.1.call-done, f32[1024]{0:T(1024)S(1)} %get-tuple-element.200, f32[1024,768]{0,1:T(8,128)S(1)} %get-tuple-element.196, f32[1024]{0:T(1024)S(1)} %broadcast_multiply_fusion.4, ...), kind=kOutput, calls=%fused_computation.125 | convolution fusion | flops 4889244672 | bytes 40938496 | tf_op jit(solution)/shard_map/dot_general | solution.py:49
  320.4 11.7 %multiply_reduce_fusion.1 = (f32[768]{0:T(1024)}, f32[1024]{0:T(1024)S(1)}, f32[1024]{0:T(1024)S(1)}, f32[768]{0:T(1024)}, f32[1024,768]{0,1:T(8,128)S(1)}) fusion(f32[1024,768]{0,1:T(8,128)} %copy-done.3, f32[1024]{0:T(1024)S(1)} %add_rsqrt_fusion.1, f32[1024]{0:T(1024)S(1)} %broadcast_multiply_fusion.5, f32[768]{0:T(1024)S(1)} %copy-done.23, ...), kind=kOutput, calls=%fused_computation.72 | convolution fusion | flops 4845989888 | bytes 22065152 | tf_op jit(solution)/shard_map/dot_general | solution.py:49
  341.9 77.7 %while.23 = (s32[]{:T(128)}, f32[2,512,2304]{2,1,0:T(8,128)}, bf16[2,512,2304]{1,2,0:T(8,128)(2,1)}, s32[2,512]{1,0:T(2,128)S(1)}, f32[2,12,512]{2,1,0:T(8,128)S...) while((s32[]{:T(128)}, f32[2,512,2304]{2,1,0:T(8,128)}, bf16[2,512,2304]{1,2,0:T(8,128)(2,1)}, ...), condition=%wide.region_14.15_spmd, body=%wide.region_12.14_spmd.sunk | while | flops 2063853568 | bytes 154589360 | solution.py:191
  419.6 10.9 %convolution_bitcast_fusion = f32[768,2304]{0,1:T(8,128)} fusion(bf16[1024,768]{1,0:T(8,128)(2,1)} %param.12, f32[1024,2304]{1,0:T(8,128)} %bitcast.148), kind=kOutput, calls=%fused_computation.59 | convolution fusion | flops 3626237952 | bytes 18087936 | tf_op jit(solution)/shard_map/dot_general | solution.py:43
  430.5 8.0 copy.98
  440.4 10.4 %fusion.48 = f32[3072,768]{1,0:T(8,128)} fusion(bf16[1024,3072]{1,0:T(8,128)(2,1)} %get-tuple-element.177, bf16[1024,768]{0,1:T(8,128)(2,1)} %copy.81, f32[1024,768]{0,1:T(8,128)S(1)} %copy-done.1, f32[1024]{0:T(1024)S(1)} %copy-done.30, f32[1024]{0:T(1024)S(1)} %copy-done.32, f32[768]{0:T(1024)S(1)} %copy-done.20, f32[1024]{0:T(1024)S(1)} %copy-done.22, ...), kind=kOutput, calls=%fused_computation.98 | convolution fusion | flops 4838916096 | bytes 20466688 | tf_op jit(solution)/shard_map/dot_general | solution.py:43
  451.4 10.6 %fusion.31 = f32[768,3072]{1,0:T(8,128)} fusion(bf16[1024,3072]{1,0:T(8,128)(2,1)} %get-tuple-element.199, f32[1024,768]{0,1:T(8,128)} %copy-done.3, f32[768]{0:T(1024)S(1)} %copy-done.36, f32[768]{0:T(1024)S(1)} %copy-done.24, f32[1024]{0:T(1024)S(1)} %copy-done.27, f32[1024]{0:T(1024)S(1)} %copy-done.18), kind=kOutput, calls=%fused_computation.75 | convolution fusion | flops 4835770368 | bytes 18888704 | tf_op jit(solution)/shard_map/dot_general | solution.py:43
  464.0 101.7 %reduce-scatter.25.cloned.1.call-done = f32[96,2304]{1,0:T(8,128)} async-done(((f32[768,2304]{1,0:T(8,128)}), f32[96,2304]{1,0:T(8,128)}) %reduce-scatter.25.cloned.1.call-update) | async-done | bytes 884752
  568.0 164.1 %reduce-scatter.23.cloned.1.call-done = f32[384,768]{1,0:T(8,128)} async-done(((f32[3072,768]{1,0:T(8,128)}), f32[384,768]{1,0:T(8,128)}) %reduce-scatter.23.cloned.1.call-update) | async-done | bytes 1179664 | tf_op jit(solution)/shard_map/reduce_scatter | solution.py:220
  736.8 11.2 %fusion.39 = f32[1024,768]{0,1:T(8,128)} fusion(f32[1024,768]{0,1:T(8,128)} %copy-done.7, bf16[768,2304]{1,0:T(8,128)(2,1)} %all-gather.6.cloned.1.call-done, f32[1024,2304]{1,0:T(8,128)} %bitcast.149), kind=kOutput, calls=%fused_computation.92 | convolution fusion | flops 3627024384 | bytes 19267584 | tf_op jit(solution)/shard_map/dot_general | solution.py:49
  758.2 140.4 %reduce-scatter.19.cloned.1.call-done = f32[96,3072]{1,0:T(8,128)} async-done(((f32[768,3072]{1,0:T(8,128)}), f32[96,3072]{1,0:T(8,128)}) %reduce-scatter.19.cloned.1.call-update) | async-done | bytes 1179664 | tf_op jit(solution)/shard_map/reduce_scatter | solution.py:219
  904.1 39.7 %all-reduce.1 = f32[9216]{0:T(1024)S(1)} all-reduce(f32[9216]{0:T(1024)S(1)} %constant_dynamic-update-slice_fusion.2), channel_id=10, replica_groups=mesh['wide'=8,'narrow'=4] {'wide','narrow'}, use_global_device_ids=true, to_apply=%region_32.33.clone | all-reduce | flops 9216 | bytes 73728
  947.7 22.4 %reduce-scatter.29.cloned.1.call-done = bf16[192,384]{1,0:T(8,128)(2,1)} async-done(((bf16[768,384]{1,0:T(8,128)(2,1)}), bf16[192,384]{1,0:T(8,128)(2,1)}) %reduce-scatter.29.cloned.1.call-update) | async-done | bytes 147472
  972.0 22.7 %reduce-scatter.21.cloned.1.call-done = bf16[96,768]{1,0:T(8,128)(2,1)} async-done(((bf16[96,3072]{1,0:T(8,128)(2,1)}), bf16[96,768]{1,0:T(8,128)(2,1)}) %reduce-scatter.21.cloned.1.call-update) | async-done | bytes 147472 | tf_op jit(solution)/shard_map/reduce_scatter | solution.py:229
  (225 shorter events, 173.4 us)
Async XLA Ops:
  7.2 26.0 %copy-start.12 = (bf16[384,192]{0,1:T(8,128)(2,1)S(1)}, bf16[384,192]{0,1:T(8,128)(2,1)}, u32[]{:S(2)}) copy-start(bf16[384,192]{0,1:T(8,128)(2,1)} %param.17) | copy-start | bytes 442372
  7.2 34.2 %copy-start.40 = (f32[288]{0:T(512)S(1)}, f32[288]{0:T(512)}, u32[]{:S(2)}) copy-start(f32[288]{0:T(512)} %param.18) | copy-start | bytes 3460
  7.2 78.6 %copy-start.8 = (bf16[1024,768]{1,0:T(8,128)(2,1)S(1)}, bf16[1024,768]{1,0:T(8,128)(2,1)}, u32[]{:S(2)}) copy-start(bf16[1024,768]{1,0:T(8,128)(2,1)} %param.19) | copy-start | bytes 4718596
  7.2 82.9 %all-gather.6.cloned.1.call-start = ((), (), s32[]{:S(2)}) async-start(), calls=%async_computation.8 | async-start | bytes 3981312 | tf_op jit(solution)/shard_map/all_gather | solution.py:122
  17.5 111.1 %all-gather.8.cloned.1.call-start = ((), (), s32[]{:S(2)}) async-start(), calls=%async_computation.9 | async-start | bytes 1327104 | tf_op jit(solution)/shard_map/all_gather | solution.py:123
  24.9 182.4 %all-gather.10.cloned.1.call-start = ((), (), s32[]{:S(2)}) async-start(), calls=%async_computation.10 | async-start | bytes 5308416 | tf_op jit(solution)/shard_map/all_gather | solution.py:124
  33.1 255.3 %all-gather.12.cloned.1.call-start = ((), (), s32[]{:S(2)}) async-start(), calls=%async_computation.11 | async-start | bytes 5308416 | tf_op jit(solution)/shard_map/all_gather | solution.py:125
  41.3 420.9 %reduce-scatter.17.cloned.1.call-start = ((), (), s32[]{:S(2)}) async-start(), calls=%async_computation.13 | async-start | bytes 2654208 | tf_op jit(solution)/shard_map/reduce_scatter | solution.py:218
  128.6 78.7 %copy-start.23 = (f32[768]{0:T(1024)S(1)}, f32[768]{0:T(1024)}, u32[]{:S(2)}) copy-start(f32[768]{0:T(1024)} %get-tuple-element.187) | copy-start | bytes 9220
  128.7 78.7 %copy-start.34 = (f32[3072]{0:T(1024)S(1)}, f32[3072]{0:T(1024)}, u32[]{:S(2)}) copy-start(f32[3072]{0:T(1024)} %slice.73) | copy-start | bytes 36868
  128.7 78.7 %copy-start.35 = (f32[768]{0:T(1024)S(1)}, f32[768]{0:T(1024)}, u32[]{:S(2)}) copy-start(f32[768]{0:T(1024)} %get-tuple-element.186) | copy-start | bytes 9220
  132.5 155.9 %copy-start.3 = (f32[1024,768]{0,1:T(8,128)}, f32[1024,768]{0,1:T(8,128)S(1)}, u32[]{:S(2)}) copy-start(f32[1024,768]{0,1:T(8,128)S(1)} %get-tuple-element.193) | copy-start | bytes 9437188
  132.5 199.5 %copy-start.17 = (f32[1024]{0:T(1024)}, f32[1024]{0:T(1024)S(1)}, u32[]{:S(2)}) copy-start(f32[1024]{0:T(1024)S(1)} %broadcast_multiply_fusion.5) | copy-start | bytes 12292
  132.9 199.1 %copy-start.26 = (f32[1024]{0:T(1024)}, f32[1024]{0:T(1024)S(1)}, u32[]{:S(2)}) copy-start(f32[1024]{0:T(1024)S(1)} %add_rsqrt_fusion.1) | copy-start | bytes 12292
  207.4 81.1 %copy-start.37 = (f32[768]{0:T(1024)S(1)}, f32[768]{0:T(1024)}, u32[]{:S(2)}) copy-start(f32[768]{0:T(1024)} %get-tuple-element.185) | copy-start | bytes 9220
  297.7 22.7 %copy-start = (f32[1024,768]{0,1:T(8,128)}, f32[1024,768]{0,1:T(8,128)S(1)}, u32[]{:S(2)}) copy-start(f32[1024,768]{0,1:T(8,128)S(1)} %get-tuple-element.196) | copy-start | bytes 9437188
  297.7 22.7 %copy-start.15 = (f32[1024]{0:T(1024)}, f32[1024]{0:T(1024)S(1)}, u32[]{:S(2)}) copy-start(f32[1024]{0:T(1024)S(1)} %broadcast_multiply_fusion.4) | copy-start | bytes 12292
  338.4 227.3 %reduce-scatter.25.cloned.1.call-start = ((), (), s32[]{:S(2)}) async-start(), calls=%async_computation.17 | async-start | bytes 7962624
  438.5 293.6 %reduce-scatter.23.cloned.1.call-start = ((), (), s32[]{:S(2)}) async-start(), calls=%async_computation.16 | async-start | bytes 10616832 | tf_op jit(solution)/shard_map/reduce_scatter | solution.py:220
  450.8 447.8 %reduce-scatter.19.cloned.1.call-start = ((), (), s32[]{:S(2)}) async-start(), calls=%async_computation.14 | async-start | bytes 10616832 | tf_op jit(solution)/shard_map/reduce_scatter | solution.py:219
  462.1 482.4 %reduce-scatter.27.cloned.1.call-start = ((), (), s32[]{:S(2)}) async-start(), calls=%async_computation.18 | async-start | bytes 245760
  464.0 482.0 %reduce-scatter.15.cloned.1.call-start = ((), (), s32[]{:S(2)}) async-start(), calls=%async_computation.12 | async-start | bytes 737280 | tf_op jit(solution)/shard_map/reduce_scatter | solution.py:223
  568.0 402.2 %reduce-scatter.29.cloned.1.call-start = ((), (), s32[]{:S(2)}) async-start(), calls=%async_computation.19 | async-start | bytes 737280
  736.4 258.3 %reduce-scatter.21.cloned.1.call-start = ((), (), s32[]{:S(2)}) async-start(), calls=%async_computation.15 | async-start | bytes 737280 | tf_op jit(solution)/shard_map/reduce_scatter | solution.py:229
  (33 other events, 173.9 us)
Sparse Core Ops, SparseCore 0:
  17.6 66.4 all-gather.5
  86.8 39.5 all-gather.7
  128.7 78.6 all-gather.9
  209.3 79.1 all-gather.11
  338.5 67.1 reduce-scatter.16
  438.6 127.0 reduce-scatter.24
  569.7 162.3 reduce-scatter.22
  736.1 162.3 reduce-scatter.18
  901.7 18.8 reduce-scatter.26
  923.1 22.3 reduce-scatter.14
  948.2 21.9 reduce-scatter.28
  972.6 22.0 reduce-scatter.20
where the time goes:
time: 1010 us; the launch traced here: 1000 us
  waiting for transfers between devices  569 us (56%)
  matrix products  181 us (18%)
  blocking collectives  113 us (11%)
  local copies, waits for them, and re-layouts  79 us (8%)
  other arithmetic  43.8 us (4%)
  between operations  15.3 us (2%)
    reduce_scatter x1, waiting for transfers between devices, per_device(): lax.psum_scatter(grad_w_back, 'wide', scatter_dimension=0, tiled=True)  164 us
    reduce_scatter x1, waiting for transfers between devices, per_device(): lax.psum_scatter(grad_w_in, 'wide', scatter_dimension=0, tiled=True)  140 us
    unnamed x15, waiting for transfers between devices  124 us
    unnamed x2, blocking collectives  82.7 us
    all_gather x1, waiting for transfers between devices, per_device(): lax.all_gather(columns[2], 'wide', axis=0, tiled=True)  74.4 us
    dot_general x4, matrix products, contract_cols(): lax.dot_general(left_side, right_side, (((1,), (1,)), ((), ())), preferre...  45.5 us
    all_gather x1, waiting for transfers between devices, per_device(): lax.all_gather(columns[3], 'wide', axis=0, tiled=True)  43.5 us
    dot_general x1, matrix products, per_device(): jnp.dot(first_low, weights_full[2], preferred_element_type=jnp.float32)  37.6 us
  transfers between devices with their start and end apart: 12, of which 7 were waited for; matrix products, arithmetic and copies ran while one was open for 25% of the time, Pallas kernels for 0%

commit v1 on v0

v1 whole, which is shorter than its diff:
```python
import functools

import jax
import jax.numpy as jnp
from jax import lax
from jax.experimental import pallas as pl
from jax.experimental.pallas import tpu as pltpu
from jax.sharding import PartitionSpec as P

D = 768
HEADS = 12
FF = 3072
ALL = ("wide", "narrow")
CHIP_STEPS = ((0, 0), (1, 0), (0, 1), (1, 1))

epsilon = 1e-06


def send(values, z=0, y=0, x=0, core=0):
    flip_wide, flip_narrow = 2 * z + y, 2 * x + core
    pairs = [
        (w * 4 + n, (w ^ flip_wide) * 4 + (n ^ flip_narrow)) for w in range(8) for n in range(4)
    ]
    return lax.ppermute(values, ALL, pairs)


def position():
    wide, narrow = lax.axis_index("wide"), lax.axis_index("narrow")
    return wide // 2, wide % 2, narrow // 2, narrow % 2


def gather_z(values):
    return jnp.stack([values] + [send(values, z=k) for k in (1, 2, 3)])


def gather_chips(lines):
    return [lines] + [send(lines, x=i, y=j) for i, j in CHIP_STEPS[1:]]


def gather_cores(blocks):
    return blocks + [send(block, core=1) for block in blocks]


def pair_kernel(*refs):
    count = len(refs) // 3
    core = lax.rem(lax.axis_index("narrow"), 2)
    for own, other, out in zip(refs[:count], refs[count : 2 * count], refs[2 * count :]):
        rows, columns = own.shape[0] // 2, own.shape[1]
        half = pl.ds(pl.multiple_of(core * rows, rows), rows)

        @pl.when(core == 0)
        def _(own=own, other=other, out=out, half=half, columns=columns):
            out[:, :columns] = own[half, :]
            out[:, columns:] = other[half, :]

        @pl.when(core == 1)
        def _(own=own, other=other, out=out, half=half, columns=columns):
            out[:, :columns] = other[half, :]
            out[:, columns:] = own[half, :]


def pair_up(*pieces):
    others = [send(piece, core=1) for piece in pieces]
    return pl.pallas_call(
        pair_kernel,
        out_shape=[
            jax.ShapeDtypeStruct((piece.shape[0] // 2, piece.shape[1] * 2), piece.dtype)
            for piece in pieces
        ],
        name="pair_up",
    )(*pieces, *others)


def assemble_kernel(widths, *refs):
    blocks, outs, sems = refs[:8], refs[8:-1], refs[-1]
    z, y, x, core = position()
    rows = blocks[0].shape[1]
    copies = []
    for other in range(2):
        for step, (i, j) in enumerate(CHIP_STEPS):
            block = blocks[other * 4 + step]
            for k in range(4):
                row = (((z ^ k) * 2 + (y ^ j)) * 2 + (core ^ other)) * rows
                left = 0
                for width, out in zip(widths, outs):
                    copies.append(
                        pltpu.make_async_copy(
                            block.at[k, :, pl.ds(left, width)],
                            out.at[
                                pl.ds(pl.multiple_of(row, rows), rows),
                                pl.ds(pl.multiple_of((x ^ i) * width, width), width),
                            ],
                            sems.at[len(copies)],
                        )
                    )
                    left += width
    for copy in copies:
        copy.start()
    for copy in copies:
        copy.wait()


def assemble(blocks, widths, name):
    rows = blocks[0].shape[1] * 16
    return pl.pallas_call(
        functools.partial(assemble_kernel, widths),
        out_shape=[jax.ShapeDtypeStruct((rows, 2 * w), blocks[0].dtype) for w in widths],
        in_specs=[pl.BlockSpec(memory_space=pl.ANY)] * 8,
        out_specs=[pl.BlockSpec(memory_space=pl.ANY)] * len(widths),
        scratch_shapes=[pltpu.SemaphoreType.DMA((32 * len(widths),))],
        name=name,
    )(*blocks)


def gather_vectors(vectors):
    z, y, x, core = position()
    lines = gather_z(vectors)
    blocks = gather_cores(gather_chips(lines))
    table = jnp.stack(blocks).reshape(2, 2, 2, 4, -1)

    def turn(values, bit, axis):
        return jnp.where(bit == 1, jnp.flip(values, axis), values)

    table = turn(turn(turn(table, core, 0), y, 1), x, 2)
    table = table.reshape(2, 2, 2, 2, 2, -1)
    table = turn(turn(table, z // 2, 3), z % 2, 4)
    return table.transpose(3, 4, 1, 2, 0, 5).reshape(-1)


def split_kernel(place, full, kept, sent, sems):
    z, y, x, core = position()
    copies = []
    for other, out in ((0, kept), (1, sent)):
        for step, (i, j) in enumerate(CHIP_STEPS):
            for k in range(4):
                row, column = place((z ^ k) * 2 + (y ^ j), x ^ i, core ^ other)
                copies.append(
                    pltpu.make_async_copy(
                        full.at[
                            pl.ds(pl.multiple_of(row, 16), out.shape[2]),
                            pl.ds(pl.multiple_of(column, 128), out.shape[3]),
                        ],
                        out.at[step, k],
                        sems.at[len(copies)],
                    )
                )
    for copy in copies:
        copy.start()
    for copy in copies:
        copy.wait()


def split_up(full, shape, place, name):
    return pl.pallas_call(
        functools.partial(split_kernel, place),
        out_shape=[jax.ShapeDtypeStruct((4, 4) + shape, full.dtype)] * 2,
        in_specs=[pl.BlockSpec(memory_space=pl.ANY)],
        out_specs=[pl.BlockSpec(memory_space=pl.ANY)] * 2,
        scratch_shapes=[pltpu.SemaphoreType.DMA((32,))],
        name=name,
    )(full)


def wide_sum(*terms):
    return functools.reduce(lambda a, b: a + b, [t.astype(jnp.float32) for t in terms])


def scatter_sum(full, shape, place, name):
    kept, sent = split_up(full, shape, place, name)
    received = send(sent, core=1)
    parts = [wide_sum(kept[s], received[s]).astype(full.dtype) for s in range(4)]
    others = [send(parts[s], x=i, y=j) for s, (i, j) in enumerate(CHIP_STEPS) if s]
    line = [
        wide_sum(parts[0][k], *[other[k] for other in others]).astype(full.dtype) for k in range(4)
    ]
    others = [send(line[k], z=k) for k in (1, 2, 3)]
    return wide_sum(line[0], *others)


def row_halves(rows, columns):
    def place(wide, x, core):
        return (wide * 2 + core) * rows, x * columns

    return place


def swap_columns(summed):
    core = lax.axis_index("narrow") % 2
    columns = summed.shape[1] // 2
    left, right = summed[:, :columns], summed[:, columns:]
    mine = jnp.where(core == 0, left, right)
    other = send(jnp.where(core == 0, right, left).astype(jnp.bfloat16), core=1).astype(jnp.float32)
    return jnp.concatenate(
        [jnp.where(core == 0, mine, other), jnp.where(core == 0, other, mine)], 0
    )


def scatter_vectors(values):
    z, y, x, core = position()
    table = values.reshape(2, 2, 2, 2, 2, -1)

    def turn(values, bit, axis):
        return jnp.where(bit == 1, jnp.flip(values, axis), values)

    for axis, bit in enumerate((z // 2, z % 2, y, x, core)):
        table = turn(table, bit, axis)
    table = table.transpose(4, 3, 2, 0, 1, 5).reshape(2, 2, 2, 4, -1)
    table = table[0] + send(table[1], core=1)
    total = table[0, 0]
    for i, j in CHIP_STEPS[1:]:
        total = total + send(table[i, j], x=i, y=j)
    own = total[0]
    for k in (1, 2, 3):
        own = own + send(total[k], z=k)
    return own


def split_vectors(vectors):
    return (
        vectors[0:D],
        vectors[D : 2 * D],
        vectors[2 * D : 3 * D],
        vectors[3 * D : 4 * D],
        vectors[4 * D : 5 * D],
        vectors[5 * D : 5 * D + FF],
        vectors[5 * D + FF : 6 * D + FF],
        vectors[6 * D + FF : 7 * D + FF],
        vectors[7 * D + FF : 8 * D + FF],
    )


def normalize(values):
    center = values - jnp.mean(values, -1, keepdims=True)
    inverse = lax.rsqrt(jnp.mean(center * center, -1, keepdims=True) + epsilon)
    return (center * inverse, inverse)


def normalize_back(grad_norm, normed, inverse):
    return inverse * (
        grad_norm
        - jnp.mean(grad_norm, -1, keepdims=True)
        - normed * jnp.mean(grad_norm * normed, -1, keepdims=True)
    )


def contract_rows(left_side, right_side):
    return lax.dot_general(
        left_side, right_side, (((0,), (0,)), ((), ())), preferred_element_type=jnp.float32
    ).astype(jnp.bfloat16)


def contract_cols(left_side, right_side):
    return lax.dot_general(
        left_side, right_side, (((1,), (1,)), ((), ())), preferred_element_type=jnp.float32
    )


def smooth(values):
    return jax.nn.gelu(values, approximate=False)


def unpack(packed):
    length = packed.shape[0]
    head_dim = packed.shape[1] // (3 * HEADS)
    shaped = packed.reshape(length, 3, HEADS, head_dim)
    return (shaped[:, 0], shaped[:, 1], shaped[:, 2])


def masked_scores(queries, key_rows, segment_row):
    score_scale = queries.shape[-1] ** (-0.5)
    scores = (
        jnp.einsum("qhd,khd->hqk", queries, key_rows, preferred_element_type=jnp.float32)
        * score_scale
    )
    same_segment = segment_row[:, None] == segment_row[None, :]
    return jnp.where(same_segment[None], scores, -1000000000.0)


def attend(block_item):
    packed, segment_row = block_item
    queries, key_rows, value_rows = unpack(packed)
    scores = masked_scores(queries, key_rows, segment_row)
    largest = jnp.max(scores, -1, keepdims=True)
    weights = jnp.exp(scores - largest)
    totals = jnp.sum(weights, -1, keepdims=True)
    probs_low = (weights / totals).astype(jnp.bfloat16)
    attended = jnp.einsum("hqk,khd->qhd", probs_low, value_rows, preferred_element_type=jnp.float32)
    logsum = (largest + jnp.log(totals))[..., 0]
    return (attended.reshape(packed.shape[0], -1).astype(jnp.bfloat16), logsum)


def attend_back(block_item):
    packed, segment_row, logsum, grad_att = block_item
    queries, key_rows, value_rows = unpack(packed)
    score_scale = queries.shape[-1] ** (-0.5)
    scores = masked_scores(queries, key_rows, segment_row)
    probs = jnp.exp(scores - logsum[..., None])
    grad_heads = grad_att.reshape(queries.shape)
    grad_probs = jnp.einsum(
        "qhd,khd->hqk", grad_heads, value_rows, preferred_element_type=jnp.float32
    )
    inner_sum = jnp.sum(probs * grad_probs, -1, keepdims=True)
    grad_scores = (probs * (grad_probs - inner_sum)).astype(jnp.bfloat16)
    grad_query = (
        jnp.einsum("hqk,khd->qhd", grad_scores, key_rows, preferred_element_type=jnp.float32)
        * score_scale
    )
    grad_key = (
        jnp.einsum("hqk,qhd->khd", grad_scores, queries, preferred_element_type=jnp.float32)
        * score_scale
    )
    grad_value = jnp.einsum(
        "hqk,qhd->khd", probs.astype(jnp.bfloat16), grad_heads, preferred_element_type=jnp.float32
    )
    return jnp.stack([grad_query, grad_key, grad_value], 1).reshape(packed.shape[0], -1)


def gather_all(trees, w_qkv, w_out, w_in, w_back, vectors):
    if not trees:

        def whole(piece):
            return lax.all_gather(
                lax.all_gather(piece, "narrow", axis=1, tiled=True), "wide", axis=0, tiled=True
            )

        full = tuple(whole(piece) for piece in (w_qkv, w_out, w_in, w_back))
        return full + (lax.all_gather(vectors, ALL, axis=0, tiled=True),)
    qkv, out, inner, back = pair_up(w_qkv, w_out, w_in, w_back)
    qkv_lines = gather_z(qkv)
    all_vectors = gather_vectors(vectors)
    qkv_lines, out, inner, back = lax.optimization_barrier((qkv_lines, out, inner, back))
    full_qkv = assemble(gather_cores(gather_chips(qkv_lines)), (1152,), "assemble_qkv")[0]
    mid_lines = gather_z(jnp.concatenate([inner, out], 1))
    back_lines = gather_z(back)
    mid = [mid_lines, send(mid_lines, x=1)]
    mid = mid + [send(block, y=1) for block in mid]
    full_in, full_out = assemble(gather_cores(mid), (1536, 384), "assemble_in")
    rear = [back_lines, send(back_lines, y=1)]
    rear = rear + [send(block, x=1) for block in rear]
    rear = [rear[0], rear[2], rear[1], rear[3]]
    full_back = assemble(gather_cores(rear), (384,), "assemble_back")[0]
    return full_qkv, full_out, full_in, full_back, all_vectors


def per_device(trees, hidden, segment, w_qkv, w_out, w_in, w_back, vectors, cotangent):
    full_qkv, full_out, full_in, full_back, all_vectors = gather_all(
        trees, w_qkv, w_out, w_in, w_back, vectors
    )
    (
        bias_query,
        bias_value,
        bias_out,
        gain_first,
        shift_first,
        bias_inner,
        bias_back,
        gain_second,
        shift_second,
    ) = split_vectors(all_vectors)
    rows_dev = segment.shape[0]
    length = segment.shape[1]
    projected = jnp.dot(hidden, full_qkv, preferred_element_type=jnp.float32)
    qkv_bias = jnp.concatenate([bias_query, jnp.zeros((D,), jnp.float32), bias_value])
    packed = (projected + qkv_bias).astype(jnp.bfloat16)
    packed_rows = packed.reshape(rows_dev, length, 3 * D)
    attended, logsum = lax.map(attend, (packed_rows, segment))
    attended = attended.reshape(rows_dev * length, D)
    branch = jnp.dot(attended, full_out, preferred_element_type=jnp.float32) + bias_out
    first_normed, first_inverse = normalize(hidden.astype(jnp.float32) + branch)
    first_out = first_normed * gain_first + shift_first
    first_low = first_out.astype(jnp.bfloat16)
    inner_act = jnp.dot(first_low, full_in, preferred_element_type=jnp.float32) + bias_inner
    activated, gelu_back = jax.vjp(smooth, inner_act)
    activated_low = activated.astype(jnp.bfloat16)
    outward = jnp.dot(activated_low, full_back, preferred_element_type=jnp.float32) + bias_back
    second_normed, second_inverse = normalize(first_out + outward)
    output = (second_normed * gain_second + shift_second).astype(jnp.bfloat16)
    grad_output = cotangent.astype(jnp.float32)
    grad_gain_second = jnp.sum(grad_output * second_normed, 0)
    grad_shift_second = jnp.sum(grad_output, 0)
    grad_second = normalize_back(grad_output * gain_second, second_normed, second_inverse)
    grad_bias_back = jnp.sum(grad_second, 0)
    second_low = grad_second.astype(jnp.bfloat16)
    grad_w_back = contract_rows(second_low, activated_low)
    grad_activated = contract_cols(second_low, full_back)
    grad_inner = gelu_back(grad_activated)[0]
    grad_bias_inner = jnp.sum(grad_inner, 0)
    inner_low = grad_inner.astype(jnp.bfloat16)
    grad_w_in = contract_rows(first_low, inner_low)
    grad_first = grad_second + contract_cols(inner_low, full_in)
    grad_gain_first = jnp.sum(grad_first * first_normed, 0)
    grad_shift_first = jnp.sum(grad_first, 0)
    grad_branch = normalize_back(grad_first * gain_first, first_normed, first_inverse)
    grad_bias_out = jnp.sum(grad_branch, 0)
    branch_low = grad_branch.astype(jnp.bfloat16)
    grad_w_out = contract_rows(attended, branch_low)
    grad_att = contract_cols(branch_low, full_out).astype(jnp.bfloat16)
    grad_packed = lax.map(
        attend_back, (packed_rows, segment, logsum, grad_att.reshape(rows_dev, length, D))
    )
    grad_packed = grad_packed.reshape(rows_dev * length, 3 * D)
    grad_bias_query = jnp.sum(grad_packed[:, :D], 0)
    grad_bias_value = jnp.sum(grad_packed[:, 2 * D :], 0)
    packed_low = grad_packed.astype(jnp.bfloat16)
    grad_w_qkv = contract_rows(hidden, packed_low)
    grad_hidden = grad_branch + contract_cols(packed_low, full_qkv)
    grad_all_vectors = jnp.concatenate(
        [
            grad_bias_query,
            grad_bias_value,
            grad_bias_out,
            grad_gain_first,
            grad_shift_first,
            grad_bias_inner,
            grad_bias_back,
            grad_gain_second,
            grad_shift_second,
        ]
    )
    if trees:
        own_back = scatter_sum(
            grad_w_back, (192, 384), lambda wide, x, core: (x * 384 + core * 192, wide * 384), "split_back"
        ).T
        own_in = scatter_sum(
            grad_w_in, (96, 768), lambda wide, x, core: (wide * 96, x * 1536 + core * 768), "split_in"
        )
        own_out = swap_columns(scatter_sum(grad_w_out, (48, 384), row_halves(48, 384), "split_out"))
        own_qkv = swap_columns(
            scatter_sum(grad_w_qkv, (48, 1152), row_halves(48, 1152), "split_qkv")
        )
        own_vectors = scatter_vectors(grad_all_vectors)
    else:

        def own(values):
            part = lax.psum_scatter(values, "wide", scatter_dimension=0, tiled=True)
            part = lax.psum_scatter(part, "narrow", scatter_dimension=1, tiled=True)
            return part.astype(jnp.float32)

        own_qkv, own_out, own_in = own(grad_w_qkv), own(grad_w_out), own(grad_w_in)
        own_back = own(grad_w_back.T)
        own_vectors = lax.psum_scatter(grad_all_vectors, ALL, scatter_dimension=0, tiled=True)
    return (output, grad_hidden, own_qkv, own_out, own_in, own_back, own_vectors)


def solution(mesh):
    trees = mesh.shape["wide"] == 8 and mesh.shape["narrow"] == 4
    return jax.shard_map(
        functools.partial(per_device, trees),
        mesh=mesh,
        in_specs=(
            P(ALL, None),
            P(ALL, None),
            P("wide", "narrow"),
            P("wide", "narrow"),
            P("wide", "narrow"),
            P("wide", "narrow"),
            P(ALL),
            P(ALL, None),
        ),
        out_specs=(
            P(ALL, None),
            P(ALL, None),
            P("wide", "narrow"),
            P("wide", "narrow"),
            P("wide", "narrow"),
            P("wide", "narrow"),
            P(ALL),
        ),
        check_vma=False,
    )
```

time: 1010 us -> 1370 us (1.36)
  Pallas kernels: 0 us -> 870 us
  waiting for transfers between devices: 569 us -> 131 us
  blocking collectives: 113 us -> 0 us
  starting transfers between devices: 0.79 us -> 80.9 us
  local copies, waits for them, and re-layouts: 79 us -> 58.8 us
    pallas_call x0 -> x8, Pallas kernels: none -> 870 us  [the longest x4 434 us: split_up(): pl.pallas_call(functools.partial(split_kernel, place), out_shape=[jax.Sha...]
    reduce_scatter x5 -> x0, waiting for transfers between devices: 327 us -> none  [the longest x1 164 us: per_device(): lax.psum_scatter(grad_w_back, 'wide', scatter_dimension=0, tiled=True)]
    ppermute x0 -> x81, waiting for transfers between devices: none -> 131 us  [send(): return lax.ppermute(values, ALL, pairs)]
    unnamed x15 -> x0, waiting for transfers between devices: 124 us -> none
    all_gather x4 -> x0, waiting for transfers between devices: 118 us -> none  [the longest x1 74.4 us: per_device(): lax.all_gather(columns[2], 'wide', axis=0, tiled=True)]
    unnamed x2 -> x0, blocking collectives: 82.7 us -> none
    ppermute x0 -> x81, starting transfers between devices: none -> 80.9 us  [send(): return lax.ppermute(values, ALL, pairs)]
    all_gather x4 -> x0, blocking collectives: 30.6 us -> none  [the longest x1 8.78 us: per_device(): lax.all_gather(w_qkv, 'narrow', axis=1, tiled=True)]
  transfers between devices with their start and end apart: 12 -> 81, of which waited for: 7 -> 36; matrix products, arithmetic and copies ran while one was open for 25% -> 6% of each run, Pallas kernels for 0% -> 39%
where the time goes in v1:
time: 1370 us
  Pallas kernels  870 us (64%)
  matrix products  180 us (13%)
  waiting for transfers between devices  131 us (10%)
  starting transfers between devices  80.9 us (6%)
  local copies, waits for them, and re-layouts  58.8 us (4%)
  other arithmetic  48.3 us (4%)
    pallas_call x4, Pallas kernels, split_up(): pl.pallas_call(functools.partial(split_kernel, place), out_shape=[jax.Sha...  434 us
    pallas_call x3, Pallas kernels, assemble(): pl.pallas_call(functools.partial(assemble_kernel, widths), out_shape=[jax...  433 us
    ppermute x81, waiting for transfers between devices, send(): return lax.ppermute(values, ALL, pairs)  131 us
    ppermute x81, starting transfers between devices, send(): return lax.ppermute(values, ALL, pairs)  80.9 us
    dot_general x1, matrix products, per_device(): jnp.dot(first_low, full_in, preferred_element_type=jnp.float32) + bias_inner  48.9 us
    dot_general x4, matrix products, contract_cols(): lax.dot_general(left_side, right_side, (((1,), (1,)), ((), ())), preferre...  45.8 us
  transfers between devices with their start and end apart: 81, of which 36 were waited for; matrix products, arithmetic and copies ran while one was open for 6% of the time, Pallas kernels for 39%

profile of v1, /device:TPU:0, one launch (start us, length us, event | category | flops | bytes accessed | tf_op | source)
XLA Modules:
  0.0 1371.9 jit_solution(11574408100019829901)
XLA Ops:
  59.5 10.5 collective-permute-done.35
  94.1 9.8 collective-permute-done.38.refs_2_
  107.6 108.6 %assemble_qkv.1 = bf16[768,2304]{1,0:T(8,128)(2,1)} custom-call(bf16[4,48,1152]{2,1,0:T(8,128)(2,1)} %copy-done.12, bf16[4,48,1152]{2,1,0:T(8,128)(2,1)} %collective-permute-done.7.refs_1_, bf16[4,48,1152]{2,1,0:T(8,128)(2,1)} %collective-permute-done.8.refs_2_, bf16[4,48,1152]{2,1,0:T(8,128)(2,1)} %collective-permute-done.9.refs_3_, ...), custom_call_target="tpu_custom_call" | custom-call | tf_op jit(solution)/shard_map/assemble_qkv/pallas_call | solution.py:105
  218.7 7.4 add_convert_fusion
  237.1 23.3 %while.22 = (s32[]{:T(128)}, bf16[2,512,768]{2,1,0:T(8,128)(2,1)}, f32[2,12,512]{2,1,0:T(8,128)S(1)}, bf16[2,512,2304]{1,2,0:T(8,128)(2,1)}, s32[2,512]{1,0:T(2,128)S(1)}, /*index=5*/s32[]{:T(128)}) while((s32[]{:T(128)}, bf16[2,512,768]{2,1,0:T(8,128)(2,1)}, f32[2,12,512]{2,1,0:T(8,128)S(1)}, bf16[2,512,2304]{1,2,0:T(8,128)(2,1)}, ...), condition=%wide.region_3.4_spmd, body=%wide.region_0.3_spmd.sunk | while | flops 843704320 | bytes 50051164 | solution.py:366
  260.4 144.3 %assemble_back.1 = bf16[3072,768]{1,0:T(8,128)(2,1)} custom-call(bf16[4,192,384]{2,1,0:T(8,128)(2,1)} %copy-done.9, bf16[4,192,384]{2,1,0:T(8,128)(2,1)} %collective-permute-done.37.refs_1_, bf16[4,192,384]{2,1,0:T(8,128)(2,1)} %copy-done.18, bf16[4,192,384]{2,1,0:T(8,128)(2,1)} %collective-permute-done.39.refs_3_, ...), custom_call_target="tpu_custom_call" | custom-call | tf_op jit(solution)/shard_map/assemble_back/pallas_call | solution.py:105
  404.8 180.4 %assemble_in.1 = (bf16[768,3072]{1,0:T(8,128)(2,1)}, bf16[768,768]{1,0:T(8,128)(2,1)}) custom-call(bf16[4,48,1920]{2,1,0:T(8,128)(2,1)} %pad_maximum_fusion.1.refs_0_, bf16[4,48,1920]{2,1,0:T(8,128)(2,1)} %collective-permute-done.27.refs_1_, bf16[4,48,1920]{2,1,0:T(8,128)(2,1)} %collective-permute-done.28.refs_2_, ...), custom_call_target="tpu_custom_call" | custom-call | tf_op jit(solution)/shard_map/assemble_in/pallas_call | solution.py:105
  589.1 48.9 %multiply_convert_fusion.1 = (bf16[1024,3072]{1,0:T(8,128)(2,1)S(1)}, f32[1024,3072]{1,0:T(8,128)}, f32[1024,3072]{1,0:T(8,128)}) fusion(f32[3072]{0:T(1024)S(1)} %copy-done.46, bf16[768,3072]{1,0:T(8,128)(2,1)S(1)} %bitcast.367, f32[1024,768]{0,1:T(8,128)S(1)} %get-tuple-element.253, f32[768]{0:T(1024)S(1)} %copy-done.48, f32[768]{0:T(1024)S(1)} %copy-done.39, ...), kind=kOutput, calls=%fused_computation.44 | convolution fusion | flops 5043388416 | bytes 39348224 | tf_op jit(solution)/shard_map/dot_general | solution.py:372
  647.3 7.4 convolution_convert_fusion.full
  654.7 20.8 %fusion.150 = (f32[3072]{0:T(1024)}, bf16[1024,3072]{1,0:T(8,128)(2,1)}) fusion(f32[1024,3072]{1,0:T(8,128)} %get-tuple-element.200, bf16[3072,768]{1,0:T(8,128)(2,1)} %assemble_back.1, f32[1024]{0:T(1024)S(1)} %get-tuple-element.260, f32[1024,768]{0,1:T(8,128)S(1)} %get-tuple-element.256, f32[1024]{0:T(1024)S(1)} %broadcast_multiply_fusion.4, ...), kind=kOutput, calls=%fused_computation.311 | convolution fusion | flops 4889244672 | bytes 40938496 | tf_op jit(solution)/shard_map/dot_general | solution.py:253
  675.6 12.1 multiply_reduce_fusion.1
  687.7 7.1 convolution_convert_fusion.1.full
  700.6 77.3 %while.23 = (s32[]{:T(128)}, f32[2,512,2304]{2,1,0:T(8,128)}, bf16[2,512,2304]{1,2,0:T(8,128)(2,1)}, s32[2,512]{1,0:T(2,128)S(1)}, f32[2,12,512]{2,1,0:T(8,128)S...) while((s32[]{:T(128)}, f32[2,512,2304]{2,1,0:T(8,128)}, bf16[2,512,2304]{1,2,0:T(8,128)(2,1)}, ...), condition=%wide.region_14.15_spmd, body=%wide.region_12.14_spmd.sunk | while | flops 2063853568 | bytes 154589360 | solution.py:398
  781.3 9.7 fusion.24.full
  793.4 37.2 %split_out.1 = (bf16[4,4,48,384]{3,2,1,0:T(8,128)(2,1)}, bf16[4,4,48,384]{3,2,1,0:T(8,128)(2,1)}) custom-call(bf16[768,768]{1,0:T(8,128)(2,1)} %convolution_convert_fusion.4.full), custom_call_target="tpu_custom_call" | custom-call | tf_op jit(solution)/shard_map/split_out/pallas_call | solution.py:154
  830.5 108.6 %split_qkv.1 = (bf16[4,4,48,1152]{3,2,1,0:T(8,128)(2,1)}, bf16[4,4,48,1152]{3,2,1,0:T(8,128)(2,1)}) custom-call(bf16[768,2304]{1,0:T(8,128)(2,1)} %fusion.24.full), custom_call_target="tpu_custom_call" | custom-call | tf_op jit(solution)/shard_map/split_qkv/pallas_call | solution.py:154
  940.9 11.3 fusion.39
  952.2 144.3 %split_back.1 = (bf16[4,4,192,384]{3,2,1,0:T(8,128)(2,1)}, bf16[4,4,192,384]{3,2,1,0:T(8,128)(2,1)}) custom-call(bf16[768,3072]{1,0:T(8,128)(2,1)} %convolution_convert_fusion.full), custom_call_target="tpu_custom_call" | custom-call | tf_op jit(solution)/shard_map/split_back/pallas_call | solution.py:154
  1096.6 144.4 %split_in.1 = (bf16[4,4,96,768]{3,2,1,0:T(8,128)(2,1)}, bf16[4,4,96,768]{3,2,1,0:T(8,128)(2,1)}) custom-call(bf16[768,3072]{1,0:T(8,128)(2,1)} %convolution_convert_fusion.1.full), custom_call_target="tpu_custom_call" | custom-call | tf_op jit(solution)/shard_map/split_in/pallas_call | solution.py:154
  1277.7 8.9 collective-permute-done.47
  1286.6 8.7 collective-permute-done.46
  1319.5 10.9 collective-permute-done.62
  1335.1 8.0 collective-permute-done.70
  1346.0 8.0 collective-permute-done.69
  (435 shorter events, 311.8 us)
Async XLA Ops:
  6.3 23.7 %collective-permute-start.1 = (bf16[96,192]{1,0:T(8,128)(2,1)}, bf16[96,192]{1,0:T(8,128)(2,1)S(1)}, u32[]{:S(2)}, u32[]{:S(2)}) collective-permute-start(bf16[96,192]{1,0:T(8,128)(2,1)} %refs_1_.1), channel_id=1, source_target_pairs={{0,1},{1,0},{2,3},{3,2},{4,5},{5,4},{6,7},{7,6},{8,9},{9,8},{10,11... | collective-permute-start | bytes 110600 | tf_op jit(solution)/shard_map/ppermute | solution.py:24
  6.3 23.7 %collective-permute-start = (bf16[96,576]{1,0:T(8,128)(2,1)}, bf16[96,576]{1,0:T(8,128)(2,1)S(1)}, u32[]{:S(2)}, u32[]{:S(2)}) collective-permute-start(bf16[96,576]{1,0:T(8,128)(2,1)} %refs_0_.1), channel_id=1, source_target_pairs={{0,1},{1,0},{2,3},{3,2},{4,5},{5,4},{6,7},{7,6},{8,9},{9,8},{10,11... | collective-permute-start | bytes 331784 | tf_op jit(solution)/shard_map/ppermute | solution.py:24
  57.4 22.5 %collective-permute-start.24 = (bf16[48,1920]{1,0:T(8,128)(2,1)S(1)}, bf16[48,1920]{1,0:T(8,128)(2,1)S(1)}, u32[]{:S(2)}, u32[]{:S(2)}) collective-permute-start(bf16[48,1920]{1,0:T(8,128)(2,1)S(1)} %constant_dynamic-update-slice_fusion.10), channel_id=1, source_target_pairs={{0,8},{1,9},{2,10},{3,11},{4,12},{5,13},{6,14},{7,15},{8,0},{9,1},... | collective-permute-start | bytes 552968 | tf_op jit(solution)/shard_map/ppermute | solution.py:24
  79.9 24.1 %collective-permute-start.38 = (bf16[4,192,384]{2,1,0:T(8,128)(2,1)S(1)}, bf16[4,192,384]{2,1,0:T(8,128)(2,1)S(1)}, u32[]{:S(2)}, u32[]{:S(2)}) collective-permute-start(bf16[4,192,384]{2,1,0:T(8,128)(2,1)S(1)} %pad_maximum_fusion.2.refs_0_), channel_id=1, source_target_pairs={{0,4},{1,5},{2,6},{3,7},{4,0},{5,1},{6,2},{7,3},{8,12},{9,13},{10,... | collective-permute-start | bytes 1769480 | tf_op jit(solution)/shard_map/ppermute | solution.py:24
  84.1 132.1 %collective-permute-start.40 = (bf16[4,192,384]{2,1,0:T(8,128)(2,1)S(1)}, bf16[4,192,384]{2,1,0:T(8,128)(2,1)}, u32[]{:S(2)}, u32[]{:S(2)}) collective-permute-start(bf16[4,192,384]{2,1,0:T(8,128)(2,1)S(1)} %pad_maximum_fusion.2.refs_0_), channel_id=1, source_target_pairs={{0,1},{1,0},{2,3},{3,2},{4,5},{5,4},{6,7},{7,6},{8,9},{9,8},{10,11... | collective-permute-start | bytes 1769480 | tf_op jit(solution)/shard_map/ppermute | solution.py:24
  91.5 126.4 %collective-permute-start.37 = (bf16[4,192,384]{2,1,0:T(8,128)(2,1)S(1)}, bf16[4,192,384]{2,1,0:T(8,128)(2,1)}, u32[]{:S(2)}, u32[]{:S(2)}) collective-permute-start(bf16[4,192,384]{2,1,0:T(8,128)(2,1)S(1)} %pad_maximum_fusion.2.refs_0_), channel_id=1, source_target_pairs={{0,2},{1,3},{2,0},{3,1},{4,6},{5,7},{6,4},{7,5},{8,10},{9,11},{10,... | collective-permute-start | bytes 1769480 | tf_op jit(solution)/shard_map/ppermute | solution.py:24
  93.0 125.1 %collective-permute-start.27 = (bf16[4,48,1920]{2,1,0:T(8,128)(2,1)}, bf16[4,48,1920]{2,1,0:T(8,128)(2,1)}, u32[]{:S(2)}, u32[]{:S(2)}) collective-permute-start(bf16[4,48,1920]{2,1,0:T(8,128)(2,1)} %pad_maximum_fusion.1.refs_0_), channel_id=1, source_target_pairs={{0,2},{1,3},{2,0},{3,1},{4,6},{5,7},{6,4},{7,5},{8,10},{9,11},{10,... | collective-permute-start | bytes 2211848 | tf_op jit(solution)/shard_map/ppermute | solution.py:24
  106.1 126.7 %collective-permute-start.28 = (bf16[4,48,1920]{2,1,0:T(8,128)(2,1)}, bf16[4,48,1920]{2,1,0:T(8,128)(2,1)}, u32[]{:S(2)}, u32[]{:S(2)}) collective-permute-start(bf16[4,48,1920]{2,1,0:T(8,128)(2,1)} %pad_maximum_fusion.1.refs_0_), channel_id=1, source_target_pairs={{0,4},{1,5},{2,6},{3,7},{4,0},{5,1},{6,2},{7,3},{8,12},{9,13},{10,... | collective-permute-start | bytes 2211848 | tf_op jit(solution)/shard_map/ppermute | solution.py:24
  107.6 125.3 %collective-permute-start.42 = (bf16[4,192,384]{2,1,0:T(8,128)(2,1)S(1)}, bf16[4,192,384]{2,1,0:T(8,128)(2,1)}, u32[]{:S(2)}, u32[]{:S(2)}) collective-permute-start(bf16[4,192,384]{2,1,0:T(8,128)(2,1)S(1)} %collective-permute-done.38.refs_2_), channel_id=1, source_target_pairs={{0,1},{1,0},{2,3},{3,2},{4,5},{5,4},{6,7},{7,6},{8,9},{9,8},{10,11... | collective-permute-start | bytes 1769480 | tf_op jit(solution)/shard_map/ppermute | solution.py:24
  232.8 172.0 %collective-permute-start.30 = (bf16[4,48,1920]{2,1,0:T(8,128)(2,1)}, bf16[4,48,1920]{2,1,0:T(8,128)(2,1)}, u32[]{:S(2)}, u32[]{:S(2)}) collective-permute-start(bf16[4,48,1920]{2,1,0:T(8,128)(2,1)} %pad_maximum_fusion.1.refs_0_), channel_id=1, source_target_pairs={{0,1},{1,0},{2,3},{3,2},{4,5},{5,4},{6,7},{7,6},{8,9},{9,8},{10,11... | collective-permute-start | bytes 2211848 | tf_op jit(solution)/shard_map/ppermute | solution.py:24
  232.9 171.8 %collective-permute-start.31 = (bf16[4,48,1920]{2,1,0:T(8,128)(2,1)}, bf16[4,48,1920]{2,1,0:T(8,128)(2,1)}, u32[]{:S(2)}, u32[]{:S(2)}) collective-permute-start(bf16[4,48,1920]{2,1,0:T(8,128)(2,1)} %collective-permute-done.27.refs_1_), channel_id=1, source_target_pairs={{0,1},{1,0},{2,3},{3,2},{4,5},{5,4},{6,7},{7,6},{8,9},{9,8},{10,11... | collective-permute-start | bytes 2211848 | tf_op jit(solution)/shard_map/ppermute | solution.py:24
  233.3 171.5 %collective-permute-start.32 = (bf16[4,48,1920]{2,1,0:T(8,128)(2,1)}, bf16[4,48,1920]{2,1,0:T(8,128)(2,1)}, u32[]{:S(2)}, u32[]{:S(2)}) collective-permute-start(bf16[4,48,1920]{2,1,0:T(8,128)(2,1)} %collective-permute-done.28.refs_2_), channel_id=1, source_target_pairs={{0,1},{1,0},{2,3},{3,2},{4,5},{5,4},{6,7},{7,6},{8,9},{9,8},{10,11... | collective-permute-start | bytes 2211848 | tf_op jit(solution)/shard_map/ppermute | solution.py:24
  233.5 26.9 %collective-permute-start.43 = (bf16[4,192,384]{2,1,0:T(8,128)(2,1)}, bf16[4,192,384]{2,1,0:T(8,128)(2,1)}, u32[]{:S(2)}, u32[]{:S(2)}) collective-permute-start(bf16[4,192,384]{2,1,0:T(8,128)(2,1)} %collective-permute-done.39.refs_3_), channel_id=1, source_target_pairs={{0,1},{1,0},{2,3},{3,2},{4,5},{5,4},{6,7},{7,6},{8,9},{9,8},{10,11... | collective-permute-start | bytes 1769480 | tf_op jit(solution)/shard_map/ppermute | solution.py:24
  237.1 167.7 %collective-permute-start.33 = (bf16[4,48,1920]{2,1,0:T(8,128)(2,1)}, bf16[4,48,1920]{2,1,0:T(8,128)(2,1)}, u32[]{:S(2)}, u32[]{:S(2)}) collective-permute-start(bf16[4,48,1920]{2,1,0:T(8,128)(2,1)} %collective-permute-done.29.refs_3_), channel_id=1, source_target_pairs={{0,1},{1,0},{2,3},{3,2},{4,5},{5,4},{6,7},{7,6},{8,9},{9,8},{10,11... | collective-permute-start | bytes 2211848 | tf_op jit(solution)/shard_map/ppermute | solution.py:24
  939.9 306.5 %collective-permute-start.74 = (f32[2,2,4,288]{3,1,2,0:T(2,128)S(1)}, f32[2,2,4,288]{3,1,2,0:T(2,128)S(1)}, u32[]{:S(2)}, u32[]{:S(2)}) collective-permute-start(f32[2,2,4,288]{3,1,2,0:T(2,128)S(1)} %bitcast.362), channel_id=1, source_target_pairs={{0,1},{1,0},{2,3},{3,2},{4,5},{5,4},{6,7},{7,6},{8,9},{9,8},{10,11... | collective-permute-start | bytes 55304 | tf_op jit(solution)/shard_map/ppermute | solution.py:24
  940.4 308.1 %collective-permute-start.52 = (bf16[4,4,48,384]{3,2,1,0:T(8,128)(2,1)}, bf16[4,4,48,384]{3,2,1,0:T(8,128)(2,1)}, u32[]{:S(2)}, u32[]{:S(2)}) collective-permute-start(bf16[4,4,48,384]{3,2,1,0:T(8,128)(2,1)} %get-tuple-element.101), channel_id=1, source_target_pairs={{0,1},{1,0},{2,3},{3,2},{4,5},{5,4},{6,7},{7,6},{8,9},{9,8},{10,11... | collective-permute-start | bytes 1769480 | tf_op jit(solution)/shard_map/ppermute | solution.py:24
  940.5 329.8 %collective-permute-start.44 = (bf16[4,4,48,1152]{3,2,1,0:T(8,128)(2,1)}, bf16[4,4,48,1152]{3,2,1,0:T(8,128)(2,1)}, u32[]{:S(2)}, u32[]{:S(2)}) collective-permute-start(bf16[4,4,48,1152]{3,2,1,0:T(8,128)(2,1)} %get-tuple-element.99), channel_id=1, source_target_pairs={{0,1},{1,0},{2,3},{3,2},{4,5},{5,4},{6,7},{7,6},{8,9},{9,8},{10,11... | collective-permute-start | bytes 5308424 | tf_op jit(solution)/shard_map/ppermute | solution.py:24
  1246.2 53.6 %collective-permute-start.60 = (bf16[4,4,96,768]{3,2,1,0:T(8,128)(2,1)}, bf16[4,4,96,768]{3,2,1,0:T(8,128)(2,1)S(1)}, u32[]{:S(2)}, u32[]{:S(2)}) collective-permute-start(bf16[4,4,96,768]{3,2,1,0:T(8,128)(2,1)} %get-tuple-element.103), channel_id=1, source_target_pairs={{0,1},{1,0},{2,3},{3,2},{4,5},{5,4},{6,7},{7,6},{8,9},{9,8},{10,11... | collective-permute-start | bytes 7077896 | tf_op jit(solution)/shard_map/ppermute | solution.py:24
  1265.4 46.2 %collective-permute-start.67 = (bf16[4,4,192,384]{3,2,1,0:T(8,128)(2,1)}, bf16[4,4,192,384]{3,2,1,0:T(8,128)(2,1)S(1)}, u32[]{:S(2)}, u32[]{:S(2)}) collective-permute-start(bf16[4,4,192,384]{3,2,1,0:T(8,128)(2,1)} %get-tuple-element.105), channel_id=1, source_target_pairs={{0,1},{1,0},{2,3},{3,2},{4,5},{5,4},{6,7},{7,6},{8,9},{9,8},{10,11... | collective-permute-start | bytes 7077896 | tf_op jit(solution)/shard_map/ppermute | solution.py:24
  1312.3 30.8 %collective-permute-start.70 = (bf16[4,192,384]{2,1,0:T(8,128)(2,1)S(1)}, bf16[4,192,384]{2,1,0:T(8,128)(2,1)S(1)}, u32[]{:S(2)}, u32[]{:S(2)}) collective-permute-start(bf16[4,192,384]{2,1,0:T(8,128)(2,1)S(1)} %get-tuple-element.206), channel_id=1, source_target_pairs={{0,6},{1,7},{2,4},{3,5},{4,2},{5,3},{6,0},{7,1},{8,14},{9,15},{10,... | collective-permute-start | bytes 1769480 | tf_op jit(solution)/shard_map/ppermute | solution.py:24
  1313.9 40.1 %collective-permute-start.69 = (bf16[4,192,384]{2,1,0:T(8,128)(2,1)S(1)}, bf16[4,192,384]{2,1,0:T(8,128)(2,1)S(1)}, u32[]{:S(2)}, u32[]{:S(2)}) collective-permute-start(bf16[4,192,384]{2,1,0:T(8,128)(2,1)S(1)} %get-tuple-element.207), channel_id=1, source_target_pairs={{0,4},{1,5},{2,6},{3,7},{4,0},{5,1},{6,2},{7,3},{8,12},{9,13},{10,... | collective-permute-start | bytes 1769480 | tf_op jit(solution)/shard_map/ppermute | solution.py:24
  1317.8 36.2 %collective-permute-start.68 = (bf16[4,192,384]{2,1,0:T(8,128)(2,1)S(1)}, bf16[4,192,384]{2,1,0:T(8,128)(2,1)S(1)}, u32[]{:S(2)}, u32[]{:S(2)}) collective-permute-start(bf16[4,192,384]{2,1,0:T(8,128)(2,1)S(1)} %get-tuple-element.208), channel_id=1, source_target_pairs={{0,2},{1,3},{2,0},{3,1},{4,6},{5,7},{6,4},{7,5},{8,10},{9,11},{10,... | collective-permute-start | bytes 1769480 | tf_op jit(solution)/shard_map/ppermute | solution.py:24
  1330.7 27.8 %collective-permute-start.64 = (bf16[96,768]{1,0:T(8,128)(2,1)S(1)}, bf16[96,768]{1,0:T(8,128)(2,1)S(1)}, u32[]{:S(2)}, u32[]{:S(2)}) collective-permute-start(bf16[96,768]{1,0:T(8,128)(2,1)S(1)} %get-tuple-element.221), channel_id=1, source_target_pairs={{0,8},{1,9},{2,10},{3,11},{4,12},{5,13},{6,14},{7,15},{8,0},{9,1},... | collective-permute-start | bytes 442376 | tf_op jit(solution)/shard_map/ppermute | solution.py:24
  1332.7 25.7 %collective-permute-start.66 = (bf16[96,768]{1,0:T(8,128)(2,1)S(1)}, bf16[96,768]{1,0:T(8,128)(2,1)S(1)}, u32[]{:S(2)}, u32[]{:S(2)}) collective-permute-start(bf16[96,768]{1,0:T(8,128)(2,1)S(1)} %get-tuple-element.222), channel_id=1, source_target_pairs={{0,24},{1,25},{2,26},{3,27},{4,28},{5,29},{6,30},{7,31},{8,16},{9,... | collective-permute-start | bytes 442376 | tf_op jit(solution)/shard_map/ppermute | solution.py:24
  (120 other events, 2931.5 us)
